TPU v7x, 512 devices: a whole 4x8x8 slice. The times are simulated.
512 devices in a mesh: blk: 64 (over y, z_hi, x), rep: 8 (over z_lo, core).
Axes of the slice: x: 4, y: 8, z: 8 (z_hi: 2, z_lo: 4; z = z_hi * 4 + z_lo), core: 2. Of those that a mesh axis runs over, the one named last changes fastest.
Arguments:
- coords: float32 [3, 65536], P(None, 'blk'), may hold values from 0 to 12, as said below
- noise: float32 [65536], P('blk'), may hold values from 0.2 to 2
- right_side: float32 [4, 65536], P(None, 'blk'), may hold values from -8 to 8
Outputs:
- solution: float32 [4, 65536], P(None, 'blk')
- residual: float32 [4, 65536], P(None, 'blk')
Inputs may be any that keep to these rules, and one draw needn't show every extreme that they name: `coords`: the first coordinate lies in [0, 12), the other two in [0, 4).
All inputs are finite; a program needn't handle non-finite values.
Results may differ from a plain program's by a relative error of at most 0.0003.
Values sent between devices are 32-bit elements; how exact they have to be, the bound alone decides.
A program may use at most 64 MiB of HBM per device.

v0:
```python
import jax
import jax.numpy as jnp
from jax import lax
from jax.sharding import PartitionSpec as P

ITERS = 2


row_block = 256


def passed_along(value, axis, by):
    count = lax.axis_size(axis)
    return lax.ppermute(value, axis, [(i, (i + by) % count) for i in range(count)])


def matern(dist_sq):
    scaled = jnp.sqrt(5.0 * dist_sq)
    return (1.0 + scaled + scaled * scaled / 3.0) * jnp.exp(-scaled)


def tile_kernel(piece, local_coords):
    dist_sq = jnp.zeros((piece.shape[1], local_coords.shape[1]), jnp.float32)
    for c in range(3):
        diff = piece[c][:, None] - local_coords[c][None, :]
        dist_sq = dist_sq + diff * diff
    return matern(dist_sq)


def block_product(remote, local_coords):
    count = remote.shape[1]
    width = min(row_block, count)
    turns = count // width

    def one_rows(k, total):
        piece = lax.dynamic_slice_in_dim(remote, k * width, width, 1)
        kernel = tile_kernel(piece, local_coords)
        return total + jnp.dot(
            piece[3:], kernel, precision=lax.Precision.HIGHEST, preferred_element_type=jnp.float32
        )

    start = jnp.zeros((remote.shape[0] - 3, local_coords.shape[1]), jnp.float32)
    return lax.fori_loop(0, turns, one_rows, start)


def kernel_full(coords, vector):
    blocks = lax.axis_size("blk")
    replicas = lax.axis_size("rep")
    steps = blocks // replicas
    rep_index = lax.axis_index("rep")
    packet = jnp.concatenate([coords, vector], axis=0)
    for bit in range((replicas - 1).bit_length()):
        moved = passed_along(packet, "blk", (1 << bit) * steps)
        packet = jnp.where(rep_index >> bit & 1 == 1, moved, packet)
    total = block_product(packet, coords)

    def turn(k, carry):
        current, summed = carry
        current = passed_along(current, "blk", 1)
        return (current, summed + block_product(current, coords))

    packet, total = lax.fori_loop(0, steps - 1, turn, (packet, total))
    return total


def local(coords, noise, right_side):

    def single_total(first):
        return lax.psum(first, "blk")

    solution = jnp.zeros_like(right_side)
    residual = right_side
    direction = right_side
    norm_now = single_total(jnp.sum(residual * residual, axis=1))
    for step in range(ITERS):
        image = lax.psum(kernel_full(coords, direction), "rep")
        image = image + noise[None, :] * direction
        alpha = norm_now / single_total(jnp.sum(direction * image, axis=1))
        solution = solution + alpha[:, None] * direction
        residual = residual - alpha[:, None] * image
        norm_next = single_total(jnp.sum(residual * residual, axis=1))
        direction = residual + (norm_next / norm_now)[:, None] * direction
        norm_now = norm_next
    return (solution, residual)


def solution(mesh):
    return jax.shard_map(
        local,
        mesh=mesh,
        in_specs=(P(None, "blk"), P("blk"), P(None, "blk")),
        out_specs=(P(None, "blk"), P(None, "blk")),
        check_vma=False,
    )
```

profile of v0, /device:TPU:2, one launch (start us, length us, event | category | flops | bytes accessed | tf_op | source)
XLA Modules:
  0.0 1062.9 jit_solution(3374010902395612823)
XLA Ops:
  1.4 3.5 collective-permute-start.2
  4.9 3.8 collective-permute-done.2
  8.7 3.0 collective-permute-start.3
  11.8 5.2 collective-permute-done.3
  17.0 7.1 collective-permute-start.4
  24.2 2.6 collective-permute-done.4
  26.7 6.9 while.84
  33.6 141.6 %while.81 = (s32[]{:T(128)}, f32[7,1024]{1,0:T(8,128)S(1)}, f32[4,1024]{1,0:T(4,128)S(1)}, f32[3,1024]{1,0:T(4,128)S(1)}, s32[]{:T(128)}, /*index=5*/s32[]{:T(12...) while((s32[]{:T(128)}, f32[7,1024]{1,0:T(8,128)S(1)}, ...), condition=%wide.region_7.8_spmd, body=%wide.region_4.7_spmd.sunk | while | flops 16527372 | bytes 304610 | solution.py:62
  33.6 3.4 collective-permute-start.1
  37.0 5.7 collective-permute-done.1
  42.7 6.9 while.86
  51.6 12.0 %collective-permute-done.1 = f32[7,1024]{1,0:T(8,128)S(1)} collective-permute-done((f32[7,1024]{1,0:T(8,128)S(1)}, f32[7,1024]{1,0:T(8,128)S(1)}, u32[]{:S(2)}, u32[]{:S(2)}) %collective-permute-start.1) | collective-permute-done | bytes 28704 | tf_op jit(solution)/shard_map/while/body/eval_jaxpr/ppermute | solution.py:14
  63.6 6.9 while.86
  72.5 12.2 %collective-permute-done.1 = f32[7,1024]{1,0:T(8,128)S(1)} collective-permute-done((f32[7,1024]{1,0:T(8,128)S(1)}, f32[7,1024]{1,0:T(8,128)S(1)}, u32[]{:S(2)}, u32[]{:S(2)}) %collective-permute-start.1) | collective-permute-done | bytes 28704 | tf_op jit(solution)/shard_map/while/body/eval_jaxpr/ppermute | solution.py:14
  84.7 6.9 while.86
  93.6 12.0 %collective-permute-done.1 = f32[7,1024]{1,0:T(8,128)S(1)} collective-permute-done((f32[7,1024]{1,0:T(8,128)S(1)}, f32[7,1024]{1,0:T(8,128)S(1)}, u32[]{:S(2)}, u32[]{:S(2)}) %collective-permute-start.1) | collective-permute-done | bytes 28704 | tf_op jit(solution)/shard_map/while/body/eval_jaxpr/ppermute | solution.py:14
  105.6 6.9 while.86
  114.5 12.0 %collective-permute-done.1 = f32[7,1024]{1,0:T(8,128)S(1)} collective-permute-done((f32[7,1024]{1,0:T(8,128)S(1)}, f32[7,1024]{1,0:T(8,128)S(1)}, u32[]{:S(2)}, u32[]{:S(2)}) %collective-permute-start.1) | collective-permute-done | bytes 28704 | tf_op jit(solution)/shard_map/while/body/eval_jaxpr/ppermute | solution.py:14
  126.5 6.9 while.86
  135.4 12.0 %collective-permute-done.1 = f32[7,1024]{1,0:T(8,128)S(1)} collective-permute-done((f32[7,1024]{1,0:T(8,128)S(1)}, f32[7,1024]{1,0:T(8,128)S(1)}, u32[]{:S(2)}, u32[]{:S(2)}) %collective-permute-start.1) | collective-permute-done | bytes 28704 | tf_op jit(solution)/shard_map/while/body/eval_jaxpr/ppermute | solution.py:14
  147.4 6.9 while.86
  156.3 12.0 %collective-permute-done.1 = f32[7,1024]{1,0:T(8,128)S(1)} collective-permute-done((f32[7,1024]{1,0:T(8,128)S(1)}, f32[7,1024]{1,0:T(8,128)S(1)}, u32[]{:S(2)}, u32[]{:S(2)}) %collective-permute-start.1) | collective-permute-done | bytes 28704 | tf_op jit(solution)/shard_map/while/body/eval_jaxpr/ppermute | solution.py:14
  168.3 6.9 while.86
  175.2 25.9 %psum.43 = f32[4,1024]{1,0:T(4,128)S(1)} all-reduce(f32[4,1024]{1,0:T(4,128)S(1)} %get-tuple-element.363), channel_id=1, replica_groups=mesh['blk'=64,'rep'=8] {'rep'}, use_global_device_ids=true, to_apply=%region_8.9 | all-reduce | flops 4096 | bytes 32768 | tf_op jit(solution)/shard_map/psum | solution.py:76
  201.3 225.0 %all-reduce = (f32[4]{0:T(128)S(1)}, f32[4]{0:T(128)S(1)}) all-reduce(f32[4]{0:T(128)S(1)} %get-tuple-element.427, f32[4]{0:T(128)S(1)} %get-tuple-element.426), channel_id=1, replica_groups=mesh['blk'=64,'rep'=8] {'blk'}, use_global_device_ids=true, to_apply=%region_1.0 | all-reduce | flops 8 | bytes 64 | tf_op jit(solution)/shard_map/psum | solution.py:69
  426.5 214.9 %psum.45 = f32[4]{0:T(128)S(1)} all-reduce(f32[4]{0:T(128)S(1)} %get-tuple-element.478), channel_id=1, replica_groups=mesh['blk'=64,'rep'=8] {'blk'}, use_global_device_ids=true, to_apply=%region_12.13 | all-reduce | flops 4 | bytes 32 | tf_op jit(solution)/shard_map/psum | solution.py:69
  643.4 5.1 collective-permute-done.5
  650.4 6.0 collective-permute-done.6
  656.4 4.7 collective-permute-start.7
  661.1 5.0 collective-permute-done.7
  666.1 6.9 while.85
  673.0 138.2 %while.83 = (s32[]{:T(128)}, f32[7,1024]{1,0:T(8,128)S(1)}, f32[4,1024]{1,0:T(4,128)S(1)}, f32[3,1024]{1,0:T(4,128)S(1)}, s32[]{:T(128)}, /*index=5*/s32[]{:T(12...) while((s32[]{:T(128)}, f32[7,1024]{1,0:T(8,128)S(1)}, ...), condition=%wide.region_18.19_spmd, body=%wide.region_15.18_spmd.sunk | while | flops 16527372 | bytes 304610 | solution.py:62
  675.0 4.0 collective-permute-done
  678.9 6.9 while.87
  687.8 12.0 %collective-permute-done = f32[7,1024]{1,0:T(8,128)S(1)} collective-permute-done((f32[7,1024]{1,0:T(8,128)S(1)}, f32[7,1024]{1,0:T(8,128)S(1)}, u32[]{:S(2)}, u32[]{:S(2)}) %collective-permute-start) | collective-permute-done | bytes 28704 | tf_op jit(solution)/shard_map/while/body/eval_jaxpr/ppermute | solution.py:14
  699.8 6.9 while.87
  708.7 12.0 %collective-permute-done = f32[7,1024]{1,0:T(8,128)S(1)} collective-permute-done((f32[7,1024]{1,0:T(8,128)S(1)}, f32[7,1024]{1,0:T(8,128)S(1)}, u32[]{:S(2)}, u32[]{:S(2)}) %collective-permute-start) | collective-permute-done | bytes 28704 | tf_op jit(solution)/shard_map/while/body/eval_jaxpr/ppermute | solution.py:14
  720.7 6.9 while.87
  729.6 12.0 %collective-permute-done = f32[7,1024]{1,0:T(8,128)S(1)} collective-permute-done((f32[7,1024]{1,0:T(8,128)S(1)}, f32[7,1024]{1,0:T(8,128)S(1)}, u32[]{:S(2)}, u32[]{:S(2)}) %collective-permute-start) | collective-permute-done | bytes 28704 | tf_op jit(solution)/shard_map/while/body/eval_jaxpr/ppermute | solution.py:14
  741.6 6.9 while.87
  750.5 12.0 %collective-permute-done = f32[7,1024]{1,0:T(8,128)S(1)} collective-permute-done((f32[7,1024]{1,0:T(8,128)S(1)}, f32[7,1024]{1,0:T(8,128)S(1)}, u32[]{:S(2)}, u32[]{:S(2)}) %collective-permute-start) | collective-permute-done | bytes 28704 | tf_op jit(solution)/shard_map/while/body/eval_jaxpr/ppermute | solution.py:14
  762.5 6.9 while.87
  771.4 12.0 %collective-permute-done = f32[7,1024]{1,0:T(8,128)S(1)} collective-permute-done((f32[7,1024]{1,0:T(8,128)S(1)}, f32[7,1024]{1,0:T(8,128)S(1)}, u32[]{:S(2)}, u32[]{:S(2)}) %collective-permute-start) | collective-permute-done | bytes 28704 | tf_op jit(solution)/shard_map/while/body/eval_jaxpr/ppermute | solution.py:14
  783.4 6.9 while.87
  792.2 12.0 %collective-permute-done = f32[7,1024]{1,0:T(8,128)S(1)} collective-permute-done((f32[7,1024]{1,0:T(8,128)S(1)}, f32[7,1024]{1,0:T(8,128)S(1)}, u32[]{:S(2)}, u32[]{:S(2)}) %collective-permute-start) | collective-permute-done | bytes 28704 | tf_op jit(solution)/shard_map/while/body/eval_jaxpr/ppermute | solution.py:14
  804.2 6.9 while.87
  811.2 25.9 %psum.46 = f32[4,1024]{1,0:T(4,128)S(1)} all-reduce(f32[4,1024]{1,0:T(4,128)S(1)} %get-tuple-element.365), channel_id=1, replica_groups=mesh['blk'=64,'rep'=8] {'rep'}, use_global_device_ids=true, to_apply=%region_19.20 | all-reduce | flops 4096 | bytes 32768 | tf_op jit(solution)/shard_map/psum | solution.py:76
  837.2 225.0 %psum.47 = f32[4]{0:T(128)S(1)} all-reduce(f32[4]{0:T(128)S(1)} %multiply_reduce_fusion), channel_id=1, replica_groups=mesh['blk'=64,'rep'=8] {'blk'}, use_global_device_ids=true, to_apply=%region_21.22 | all-reduce | flops 4 | bytes 32 | tf_op jit(solution)/shard_map/psum | solution.py:69
  (273 shorter events, 140.9 us)
Async XLA Ops:
  0.6 8.1 copy-start
  0.6 8.1 copy-start.1
  1.4 7.3 collective-permute-start.2
  8.7 8.3 collective-permute-start.3
  17.0 9.7 collective-permute-start.4
  33.6 9.1 collective-permute-start.1
  49.7 13.9 %collective-permute-start.1 = (f32[7,1024]{1,0:T(8,128)S(1)}, f32[7,1024]{1,0:T(8,128)S(1)}, u32[]{:S(2)}, u32[]{:S(2)}) collective-permute-start(f32[7,1024]{1,0:T(8,128)S(1)} %get-tuple-element.839), channel_id=1, source_target_pairs={{0,8},{8,16},{16,24},{24,32},{32,40},{40,48},{48,56},{56,64},{64,7... | collective-permute-start | bytes 86024 | tf_op jit(solution)/shard_map/while/body/eval_jaxpr/ppermute | solution.py:14
  70.6 14.1 %collective-permute-start.1 = (f32[7,1024]{1,0:T(8,128)S(1)}, f32[7,1024]{1,0:T(8,128)S(1)}, u32[]{:S(2)}, u32[]{:S(2)}) collective-permute-start(f32[7,1024]{1,0:T(8,128)S(1)} %get-tuple-element.839), channel_id=1, source_target_pairs={{0,8},{8,16},{16,24},{24,32},{32,40},{40,48},{48,56},{56,64},{64,7... | collective-permute-start | bytes 86024 | tf_op jit(solution)/shard_map/while/body/eval_jaxpr/ppermute | solution.py:14
  91.7 13.9 %collective-permute-start.1 = (f32[7,1024]{1,0:T(8,128)S(1)}, f32[7,1024]{1,0:T(8,128)S(1)}, u32[]{:S(2)}, u32[]{:S(2)}) collective-permute-start(f32[7,1024]{1,0:T(8,128)S(1)} %get-tuple-element.839), channel_id=1, source_target_pairs={{0,8},{8,16},{16,24},{24,32},{32,40},{40,48},{48,56},{56,64},{64,7... | collective-permute-start | bytes 86024 | tf_op jit(solution)/shard_map/while/body/eval_jaxpr/ppermute | solution.py:14
  112.5 13.9 %collective-permute-start.1 = (f32[7,1024]{1,0:T(8,128)S(1)}, f32[7,1024]{1,0:T(8,128)S(1)}, u32[]{:S(2)}, u32[]{:S(2)}) collective-permute-start(f32[7,1024]{1,0:T(8,128)S(1)} %get-tuple-element.839), channel_id=1, source_target_pairs={{0,8},{8,16},{16,24},{24,32},{32,40},{40,48},{48,56},{56,64},{64,7... | collective-permute-start | bytes 86024 | tf_op jit(solution)/shard_map/while/body/eval_jaxpr/ppermute | solution.py:14
  133.4 13.9 %collective-permute-start.1 = (f32[7,1024]{1,0:T(8,128)S(1)}, f32[7,1024]{1,0:T(8,128)S(1)}, u32[]{:S(2)}, u32[]{:S(2)}) collective-permute-start(f32[7,1024]{1,0:T(8,128)S(1)} %get-tuple-element.839), channel_id=1, source_target_pairs={{0,8},{8,16},{16,24},{24,32},{32,40},{40,48},{48,56},{56,64},{64,7... | collective-permute-start | bytes 86024 | tf_op jit(solution)/shard_map/while/body/eval_jaxpr/ppermute | solution.py:14
  154.3 13.9 %collective-permute-start.1 = (f32[7,1024]{1,0:T(8,128)S(1)}, f32[7,1024]{1,0:T(8,128)S(1)}, u32[]{:S(2)}, u32[]{:S(2)}) collective-permute-start(f32[7,1024]{1,0:T(8,128)S(1)} %get-tuple-element.839), channel_id=1, source_target_pairs={{0,8},{8,16},{16,24},{24,32},{32,40},{40,48},{48,56},{56,64},{64,7... | collective-permute-start | bytes 86024 | tf_op jit(solution)/shard_map/while/body/eval_jaxpr/ppermute | solution.py:14
  175.2 25.9 %copy-start.2 = (f32[1024]{0:T(1024)S(1)}, f32[1024]{0:T(1024)}, u32[]{:S(2)}) copy-start(f32[1024]{0:T(1024)} %param.16) | copy-start | bytes 12292
  641.4 7.0 collective-permute-start.5
  648.5 7.9 collective-permute-start.6
  656.4 9.7 collective-permute-start.7
  673.0 5.9 collective-permute-start
  685.9 13.9 %collective-permute-start = (f32[7,1024]{1,0:T(8,128)S(1)}, f32[7,1024]{1,0:T(8,128)S(1)}, u32[]{:S(2)}, u32[]{:S(2)}) collective-permute-start(f32[7,1024]{1,0:T(8,128)S(1)} %get-tuple-element.911), channel_id=1, source_target_pairs={{0,8},{8,16},{16,24},{24,32},{32,40},{40,48},{48,56},{56,64},{64,7... | collective-permute-start | bytes 86024 | tf_op jit(solution)/shard_map/while/body/eval_jaxpr/ppermute | solution.py:14
  706.8 13.9 %collective-permute-start = (f32[7,1024]{1,0:T(8,128)S(1)}, f32[7,1024]{1,0:T(8,128)S(1)}, u32[]{:S(2)}, u32[]{:S(2)}) collective-permute-start(f32[7,1024]{1,0:T(8,128)S(1)} %get-tuple-element.911), channel_id=1, source_target_pairs={{0,8},{8,16},{16,24},{24,32},{32,40},{40,48},{48,56},{56,64},{64,7... | collective-permute-start | bytes 86024 | tf_op jit(solution)/shard_map/while/body/eval_jaxpr/ppermute | solution.py:14
  727.6 13.9 %collective-permute-start = (f32[7,1024]{1,0:T(8,128)S(1)}, f32[7,1024]{1,0:T(8,128)S(1)}, u32[]{:S(2)}, u32[]{:S(2)}) collective-permute-start(f32[7,1024]{1,0:T(8,128)S(1)} %get-tuple-element.911), channel_id=1, source_target_pairs={{0,8},{8,16},{16,24},{24,32},{32,40},{40,48},{48,56},{56,64},{64,7... | collective-permute-start | bytes 86024 | tf_op jit(solution)/shard_map/while/body/eval_jaxpr/ppermute | solution.py:14
  748.5 13.9 %collective-permute-start = (f32[7,1024]{1,0:T(8,128)S(1)}, f32[7,1024]{1,0:T(8,128)S(1)}, u32[]{:S(2)}, u32[]{:S(2)}) collective-permute-start(f32[7,1024]{1,0:T(8,128)S(1)} %get-tuple-element.911), channel_id=1, source_target_pairs={{0,8},{8,16},{16,24},{24,32},{32,40},{40,48},{48,56},{56,64},{64,7... | collective-permute-start | bytes 86024 | tf_op jit(solution)/shard_map/while/body/eval_jaxpr/ppermute | solution.py:14
  769.4 13.9 %collective-permute-start = (f32[7,1024]{1,0:T(8,128)S(1)}, f32[7,1024]{1,0:T(8,128)S(1)}, u32[]{:S(2)}, u32[]{:S(2)}) collective-permute-start(f32[7,1024]{1,0:T(8,128)S(1)} %get-tuple-element.911), channel_id=1, source_target_pairs={{0,8},{8,16},{16,24},{24,32},{32,40},{40,48},{48,56},{56,64},{64,7... | collective-permute-start | bytes 86024 | tf_op jit(solution)/shard_map/while/body/eval_jaxpr/ppermute | solution.py:14
  790.3 13.9 %collective-permute-start = (f32[7,1024]{1,0:T(8,128)S(1)}, f32[7,1024]{1,0:T(8,128)S(1)}, u32[]{:S(2)}, u32[]{:S(2)}) collective-permute-start(f32[7,1024]{1,0:T(8,128)S(1)} %get-tuple-element.911), channel_id=1, source_target_pairs={{0,8},{8,16},{16,24},{24,32},{32,40},{40,48},{48,56},{56,64},{64,7... | collective-permute-start | bytes 86024 | tf_op jit(solution)/shard_map/while/body/eval_jaxpr/ppermute | solution.py:14
where the time goes:
time: 1060 us
  blocking collectives  717 us (68%)
  waiting for transfers between devices  181 us (17%)
  matrix products  104 us (10%)
  starting transfers between devices  50.6 us (5%)
    psum x3, blocking collectives, single_total(): return lax.psum(first, 'blk')  665 us
    ppermute x20, waiting for transfers between devices, passed_along(): lax.ppermute(value, axis, [(i, (i + by) % count) for i in range(count)])  181 us
    dot_general x64, matrix products, one_rows(): jnp.dot(piece[3:], kernel, precision=lax.Precision.HIGHEST, preferred_ele...  104 us
    psum x2, blocking collectives, local(): image = lax.psum(kernel_full(coords, direction), 'rep')  51.8 us
    ppermute x20, starting transfers between devices, passed_along(): lax.ppermute(value, axis, [(i, (i + by) % count) for i in range(count)])  50.6 us
  transfers between devices with their start and end apart: 20, of which 20 were waited for; matrix products, arithmetic and copies ran while one was open for 0% of the time, Pallas kernels for 0%

commit v1 on v0

v1 whole, which is shorter than its diff:
```python
import functools
import math

import jax
import jax.numpy as jnp
from jax import lax
from jax.experimental import pallas as pl
from jax.experimental.pallas import tpu as pltpu
from jax.sharding import PartitionSpec as P

F32 = jnp.float32
BF16 = jnp.bfloat16
MESH = pl.DeviceIdType.MESH

LN2 = math.log(2.0)
SCALE = math.sqrt(5.0) / LN2
LINEAR = 3.0 / LN2
CONST = 3.0 / (LN2 * LN2)
OUTER = LN2 * LN2 / 3.0
TINY = 1e-30

BLOCK = 1024
NEAR = 8
REPS = 8
DY = (0, 1, -1, 2, -2, 3, -3, 4)


def place():
    b = lax.axis_index("blk")
    p = lax.axis_index("rep")
    return b // 8, (b // 4) % 2, b % 4, p // 2, p % 2


def device(y, zh, x, zl, c):
    return ((y * 2 + zh) * 4 + x, zl * 2 + c)


def partner(k, sign):
    y, zh, x, zl, c = place()
    outer = 1 - ((zl + 1) // 2) % 2
    other_zl = zl + outer * (3 - 2 * zl)
    other_zh = zh + outer * (1 - 2 * zh)
    reader = zl if sign > 0 else other_zl
    dx = (reader // 2 * 2 + c + k) % 4
    return device((y + sign * DY[k] + 8) % 8, other_zh, (x + sign * dx + 4) % 4, other_zl, c)


def rep_peer(k):
    return (lax.axis_index("blk"), (lax.axis_index("rep") + k) % REPS)


def y_peer(k):
    y, zh, x, zl, c = place()
    return device((y + k) % 8, zh, x, zl, c)


def zx_peer(k):
    y, zh, x, zl, c = place()
    zh_move, dx = k // 4, k % 4
    if zh_move:
        return device(y, 1 - zh, (x + dx) % 4, 3 - zl, c)
    return device(y, zh, (x + dx) % 4, zl, c)


def parts3(value):
    a = value.astype(BF16).astype(F32)
    rest = value - a
    b = rest.astype(BF16).astype(F32)
    c = (rest - b).astype(BF16).astype(F32)
    return a, b, c


PAIRS = ((0, 0), (0, 1), (0, 2), (1, 0), (1, 1), (2, 0))


def augmented(places, own):
    row = lax.broadcasted_iota(jnp.int32, (8, places.shape[1]), 0)
    parts = parts3(jnp.where(row < 4, places, 0.0))
    groups = []
    for a, b in PAIRS:
        if own:
            part = parts[b]
            length = jnp.broadcast_to(part[3:4], part.shape)
            group = jnp.where(row < 3, part, 0.0)
            group = jnp.where(row == 3, 1.0 if b == 0 else 0.0, group)
            group = jnp.where(row == 4, length if a == 0 else 0.0, group)
        else:
            part = parts[a]
            group = jnp.where(row < 3, -2.0 * part, jnp.where(row == 3, part if b == 0 else 0.0, 0.0))
            group = jnp.where(row == 4, 1.0 if a == 0 else 0.0, group)
        groups.append(group)
    groups.append(jnp.zeros((128 - 8 * len(PAIRS), places.shape[1]), F32))
    return jnp.concatenate(groups, axis=0)


def two_terms(vector):
    lead = vector.astype(BF16).astype(F32)
    return jnp.concatenate([lead, vector - lead, jnp.zeros((8, vector.shape[1]), F32)], axis=0).astype(BF16)


def matmul(a, b):
    return jnp.dot(a, b, preferred_element_type=F32)


def kernel(coords, noise, right, x_out, res_out, packet, packets, high, low, own_aug, part1, image1, images, part2,
           sums, sums_y, sums_zx, send, recv):
    y, zh, x, zl, c = place()
    rep = lax.axis_index("rep")
    own_first = jnp.logical_and(zl == 1, c == 0)

    def copy(src, dst, index, to):
        return pltpu.make_async_remote_copy(
            src_ref=src, dst_ref=dst, send_sem=send.at[index], recv_sem=recv.at[index], device_id=to,
            device_id_type=MESH,
        )

    barrier = pltpu.get_barrier_semaphore()
    for k in range(1, REPS):
        pl.semaphore_signal(barrier, inc=1, device_id=rep_peer(k), device_id_type=MESH)
    for k in range(1, NEAR):
        pl.semaphore_signal(barrier, inc=1, device_id=partner(k, 1), device_id_type=MESH)

    @pl.when(jnp.logical_not(own_first))
    def _():
        pl.semaphore_signal(barrier, inc=1, device_id=partner(0, 1), device_id_type=MESH)

    along = lax.broadcasted_iota(jnp.int32, (3, BLOCK), 0)
    centred = (coords[...] - jnp.where(along == 0, 6.0, 2.0)) * SCALE
    packet[0:3] = centred
    packet[3:4] = jnp.sum(centred * centred, axis=0, keepdims=True)
    packet[4:8] = right[...]
    own_aug[...] = augmented(packet[...], True).astype(BF16)

    @pl.when(own_first)
    def _():
        pl.semaphore_wait(barrier, NEAR + REPS - 2)
        packets[0] = packet[...]

    @pl.when(jnp.logical_not(own_first))
    def _():
        pl.semaphore_wait(barrier, NEAR + REPS - 1)
        copy(packet, packets.at[0], 0, partner(0, -1)).start()

    for k in range(1, NEAR):
        copy(packet, packets.at[k], k, partner(k, -1)).start()

    def wait_near(buffers, k, base):
        @pl.when(jnp.logical_not(jnp.logical_and(own_first, k == 0)))
        def _():
            copy(buffers.at[k], buffers.at[k], base + k, rep_peer(1)).wait_recv()

    def build(k, total):
        wait_near(packets, k, 0)
        block = packets[k]
        remote = augmented(block, False).T.astype(BF16)
        dist = jnp.maximum(matmul(remote, own_aug[...]), TINY)
        t = dist * lax.rsqrt(dist)
        value = ((t + LINEAR) * t + CONST) * jnp.exp2(-t)
        lead = value.astype(BF16)
        rest = (value - lead.astype(F32)).astype(BF16)
        rows = pl.ds(pl.multiple_of(k * BLOCK, BLOCK), BLOCK)
        high[rows, :] = lead
        low[rows, :] = rest
        vector = two_terms(block[4:8] * OUTER)
        return total + matmul(vector, lead) + matmul(vector, rest)

    def again(k, total):
        wait_near(images, k, NEAR + REPS)
        rows = pl.ds(pl.multiple_of(k * BLOCK, BLOCK), BLOCK)
        vector = two_terms(images[k] * OUTER)
        return total + matmul(vector, high[rows, :]) + matmul(vector, low[rows, :])

    def over_reps(part, total, base):
        part[rep] = total[0:4] + total[4:8]
        for k in range(1, REPS):
            copy(part.at[rep], part.at[rep], base + k, rep_peer(k)).start()
        for k in range(1, REPS):
            copy(part.at[rep], part.at[rep], base + k, rep_peer(k)).wait_recv()
        whole = part[0]
        for q in range(1, REPS):
            whole = whole + part[q]
        return whole

    zeros = jnp.zeros((16, BLOCK), F32)
    r0 = right[...]
    total = lax.fori_loop(0, NEAR, build, zeros)
    w1 = over_reps(part1, total, NEAR) + noise[...] * r0
    image1[...] = w1

    base = NEAR + REPS
    for k in range(1, NEAR):
        copy(image1, images.at[k], base + k, partner(k, -1)).start()

    @pl.when(own_first)
    def _():
        images[0] = image1[...]

    @pl.when(jnp.logical_not(own_first))
    def _():
        copy(image1, images.at[0], base, partner(0, -1)).start()

    total = lax.fori_loop(0, NEAR, again, zeros)
    w1 = image1[...]
    w2 = over_reps(part2, total, base + NEAR) + noise[...] * w1

    lane = lax.broadcasted_iota(jnp.int32, (4, 128), 1)
    grams = jnp.zeros((4, 128), F32)
    for at, (left, other) in enumerate(((r0, r0), (r0, w1), (w1, w1), (r0, w2), (w1, w2))):
        grams = jnp.where(lane == at, jnp.sum(left * other, axis=1, keepdims=True), grams)
    base = base + NEAR + REPS
    b = lax.axis_index("blk")

    sums_y[y] = grams
    for k in range(1, 8):
        copy(sums_y.at[y], sums_y.at[y], base + k, y_peer(k)).start()
    for k in range(1, 8):
        copy(sums_y.at[y], sums_y.at[y], base + k, y_peer(k)).wait_recv()
    grams = sums_y[0]
    for q in range(1, 8):
        grams = grams + sums_y[q]

    base = base + 8
    mine = b % 8
    sums_zx[mine] = grams
    for k in range(1, 8):
        copy(sums_zx.at[mine], sums_zx.at[mine], base + k, zx_peer(k)).start()
    for k in range(1, 8):
        copy(sums_zx.at[mine], sums_zx.at[mine], base + k, zx_peer(k)).wait_recv()
    grams = sums_zx[0]
    for q in range(1, 8):
        grams = grams + sums_zx[q]

    g00, g01, g11, g02, g12 = (grams[:, at:at + 1] for at in range(5))
    alpha = g00 / g01
    new = g00 - 2.0 * alpha * g01 + alpha * alpha * g11
    more = 1.0 + new / g00
    bottom = more * more * g01 - alpha * more * (g02 + g11) + alpha * alpha * g12
    alpha2 = new / bottom
    direction = more * r0 - alpha * w1
    image = more * w1 - alpha * w2
    x_out[...] = alpha * r0 + alpha2 * direction
    res_out[...] = (r0 - alpha * w1) - alpha2 * image

    for k in range(1, NEAR):
        copy(packet, packets.at[k], k, partner(k, -1)).wait_send()
        copy(image1, images.at[k], NEAR + REPS + k, partner(k, -1)).wait_send()

    @pl.when(jnp.logical_not(own_first))
    def _():
        copy(packet, packets.at[0], 0, partner(0, -1)).wait_send()
        copy(image1, images.at[0], NEAR + REPS, partner(0, -1)).wait_send()

    for k in range(1, REPS):
        copy(part1.at[rep], part1.at[rep], NEAR + k, rep_peer(k)).wait_send()
        copy(part2.at[rep], part2.at[rep], 2 * NEAR + REPS + k, rep_peer(k)).wait_send()
    for k in range(1, 8):
        copy(sums_y.at[y], sums_y.at[y], 2 * (NEAR + REPS) + k, y_peer(k)).wait_send()
        copy(sums_zx.at[mine], sums_zx.at[mine], 2 * (NEAR + REPS) + 8 + k, zx_peer(k)).wait_send()


def local(coords, noise, right_side):
    vmem = pl.BlockSpec(memory_space=pltpu.VMEM)
    field = jax.ShapeDtypeStruct((4, BLOCK), F32)
    copies = 2 * (NEAR + REPS) + 16
    call = pl.pallas_call(
        kernel,
        out_shape=(field, field),
        in_specs=[vmem] * 3,
        out_specs=(vmem, vmem),
        scratch_shapes=[
            pltpu.VMEM((8, BLOCK), F32),
            pltpu.VMEM((NEAR, 8, BLOCK), F32),
            pltpu.VMEM((NEAR * BLOCK, BLOCK), BF16),
            pltpu.VMEM((NEAR * BLOCK, BLOCK), BF16),
            pltpu.VMEM((128, BLOCK), BF16),
            pltpu.VMEM((REPS, 4, BLOCK), F32),
            pltpu.VMEM((4, BLOCK), F32),
            pltpu.VMEM((NEAR, 4, BLOCK), F32),
            pltpu.VMEM((REPS, 4, BLOCK), F32),
            pltpu.VMEM((4, 128), F32),
            pltpu.VMEM((8, 4, 128), F32),
            pltpu.VMEM((8, 4, 128), F32),
            pltpu.SemaphoreType.DMA((copies,)),
            pltpu.SemaphoreType.DMA((copies,)),
        ],
        compiler_params=pltpu.CompilerParams(
            collective_id=0, has_side_effects=True, vmem_limit_bytes=60 * 1024 * 1024
        ),
    )
    return call(coords, noise[None, :], right_side)


def solution(mesh):
    return jax.shard_map(
        local,
        mesh=mesh,
        in_specs=(P(None, "blk"), P("blk"), P(None, "blk")),
        out_specs=(P(None, "blk"), P(None, "blk")),
        check_vma=False,
    )
```

time: 1060 us -> 76.8 us (0.07)
  the two profiles are of different devices: /device:TPU:2 before, /device:TPU:1 now
where the time goes in v1:
time: 76.8 us; the launch traced here: 76.6 us
  Pallas kernels  74 us (96%)
  local copies, waits for them, and re-layouts  1.94 us (3%)
    pallas_call x1, Pallas kernels, local(): return call(coords, noise[None, :], right_side)  74 us
    unnamed x4, local copies, waits for them, and re-layouts  1.94 us

profile of v1, /device:TPU:1, one launch (start us, length us, event | category | flops | bytes accessed | tf_op | source)
XLA Modules:
  0.0 76.6 jit_solution(13819595000914239085)
XLA Ops:
  0.6 74.0 %shard_map.50 = (f32[4,1024]{1,0:T(4,128)}, f32[4,1024]{1,0:T(4,128)}) custom-call(f32[3,1024]{1,0:T(4,128)} %coords.1, f32[1,1024]{1,0:T(1,128)} %bitcast.1, f32[4,1024]{1,0:T(4,128)} %right.1), custom_call_target="tpu_custom_call" | custom-call | tf_op jit(solution)/shard_map/pallas_call | solution.py:290
  74.6 0.0 copy-start
  74.6 1.3 %copy.7 = f32[4,1024]{1,0:T(4,128)} copy(f32[4,1024]{1,0:T(4,128)} %get-tuple-element.4) | data formatting | bytes 32768
  76.0 0.0 copy-done
  76.0 0.6 copy.8
Async XLA Ops:
  74.6 1.3 %copy-start = (f32[4,1024]{1,0:T(4,128)S(1)}, f32[4,1024]{1,0:T(4,128)}, u32[]{:S(2)}) copy-start(f32[4,1024]{1,0:T(4,128)} %get-tuple-element.5) | copy-start | bytes 49156

commit v2 on v1

v2 whole, which is shorter than its diff:
```python
import functools
import math

import jax
import jax.numpy as jnp
from jax import lax
from jax.experimental import pallas as pl
from jax.experimental.pallas import tpu as pltpu
from jax.sharding import PartitionSpec as P

F32 = jnp.float32
BF16 = jnp.bfloat16
MESH = pl.DeviceIdType.MESH

LN2 = math.log(2.0)
SCALE = math.sqrt(5.0) / LN2
LINEAR = 3.0 / LN2
CONST = 3.0 / (LN2 * LN2)
OUTER = LN2 * LN2 / 3.0
TINY = 1e-30

BLOCK = 1024
NEAR = 8
WHOLE = 4
PARTS = 4
WIDTH = BLOCK // PARTS
REPS = 8
DY = (0, 1, -1, 2, -2, 3, -3, 4)


def place():
    b = lax.axis_index("blk")
    p = lax.axis_index("rep")
    return b // 8, (b // 4) % 2, b % 4, p // 2, p % 2


def device(y, zh, x, zl, c):
    return ((y * 2 + zh) * 4 + x, zl * 2 + c)


def partner(k, sign, relayed=False):
    y, zh, x, zl, c = place()
    outer = 0 if relayed else 1 - ((zl + 1) // 2) % 2
    other_zl = zl + outer * (3 - 2 * zl)
    other_zh = zh + outer * (1 - 2 * zh)
    reader = zl if sign > 0 else other_zl
    dx = (reader // 2 * 2 + c + k) % 4
    return device((y + sign * DY[k] + 8) % 8, other_zh, (x + sign * dx + 4) % 4, other_zl, c)


def over_border():
    y, zh, x, zl, c = place()
    return device(y, 1 - zh, x, 3 - zl, c)


def rep_peer(k):
    return (lax.axis_index("blk"), (lax.axis_index("rep") + k) % REPS)


def y_peer(k):
    y, zh, x, zl, c = place()
    return device((y + k) % 8, zh, x, zl, c)


def zx_peer(k):
    y, zh, x, zl, c = place()
    zh_move, dx = k // 4, k % 4
    if zh_move:
        return device(y, 1 - zh, (x + dx) % 4, 3 - zl, c)
    return device(y, zh, (x + dx) % 4, zl, c)


def parts3(value):
    a = value.astype(BF16).astype(F32)
    rest = value - a
    b = rest.astype(BF16).astype(F32)
    c = (rest - b).astype(BF16).astype(F32)
    return a, b, c


PAIRS = ((0, 0), (0, 1), (0, 2), (1, 0), (1, 1), (2, 0))


def augmented(places, own):
    row = lax.broadcasted_iota(jnp.int32, (8, places.shape[1]), 0)
    parts = parts3(jnp.where(row < 4, places, 0.0))
    groups = []
    for a, b in PAIRS:
        if own:
            part = parts[b]
            length = jnp.broadcast_to(part[3:4], part.shape)
            group = jnp.where(row < 3, part, 0.0)
            group = jnp.where(row == 3, 1.0 if b == 0 else 0.0, group)
            group = jnp.where(row == 4, length if a == 0 else 0.0, group)
        else:
            part = parts[a]
            group = jnp.where(row < 3, -2.0 * part, jnp.where(row == 3, part if b == 0 else 0.0, 0.0))
            group = jnp.where(row == 4, 1.0 if a == 0 else 0.0, group)
        groups.append(group)
    groups.append(jnp.zeros((128 - 8 * len(PAIRS), places.shape[1]), F32))
    return jnp.concatenate(groups, axis=0)


def two_terms(vector):
    lead = vector.astype(BF16).astype(F32)
    return jnp.concatenate([lead, vector - lead, jnp.zeros((8, vector.shape[1]), F32)], axis=0).astype(BF16)


def matmul(a, b):
    return jnp.dot(a, b, preferred_element_type=F32)


def kernel(coords_in, noise_in, right_in, out, packet, origin, packets, high, low, own_aug, remote_aug, partial, part1,
           image1, images, part2, sums_rep, sums_y, sums_zx, send_near, recv_near, send1, recv1, send_image, recv_image,
           send_end, recv_end, coords, noise, right, load):
    y, zh, x, zl, c = place()
    rep = lax.axis_index("rep")
    own_first = jnp.logical_and(zl == 1, c == 0)
    not_own = jnp.logical_not(own_first)
    outer = 1 - ((zl + 1) // 2) % 2
    group_first = zl // 2 * 2 + c == 0
    not_group = jnp.logical_not(group_first)

    def copy(src, dst, sent, received, to):
        return pltpu.make_async_remote_copy(
            src_ref=src, dst_ref=dst, send_sem=sent, recv_sem=received, device_id=to, device_id_type=MESH
        )

    barrier = pltpu.get_barrier_semaphore()
    @pl.when(outer == 1)
    def _():
        pl.semaphore_signal(barrier, inc=1, device_id=over_border(), device_id_type=MESH)

    for k in range(1, NEAR):
        pl.semaphore_signal(barrier, inc=1, device_id=partner(k, 1, True), device_id_type=MESH)

    @pl.when(not_group)
    def _():
        pl.semaphore_signal(barrier, inc=1, device_id=partner(0, 1, True), device_id_type=MESH)

    for k in range(1, REPS):
        pl.semaphore_signal(barrier, inc=1, device_id=rep_peer(k), device_id_type=MESH)

    loads = [
        pltpu.make_async_copy(given, held_here, load.at[at])
        for at, (given, held_here) in enumerate(((coords_in, coords), (right_in, right), (noise_in, noise)))
    ]
    for one in loads:
        one.start()
    for one in loads:
        one.wait()
    along = lax.broadcasted_iota(jnp.int32, (3, BLOCK), 0)
    centred = (coords[...] - jnp.where(along == 0, 6.0, 2.0)) * SCALE
    packet[0:3] = centred
    packet[3:4] = jnp.sum(centred * centred, axis=0, keepdims=True)
    packet[4:8] = right[...]

    def near_copy(k):
        return copy(origin, packets.at[k], send_near.at[k], recv_near.at[k], partner(k, -1, True))

    def image_copy(q, k):
        return copy(image1.at[q], images.at[q, k], send_image.at[q, k], recv_image.at[q, k], partner(k, -1))

    def part_copy(q, k):
        return copy(part1.at[q, rep], part1.at[q, rep], send1.at[q, k], recv1.at[q, k], rep_peer(k))

    def crossing():
        return copy(packet, origin, send_near.at[NEAR], recv_near.at[NEAR], over_border())

    signals = NEAR + REPS - 1

    @pl.when(jnp.logical_and(outer == 0, group_first))
    def _():
        pl.semaphore_wait(barrier, signals - 1)

    @pl.when(jnp.logical_and(outer == 0, not_group))
    def _():
        pl.semaphore_wait(barrier, signals)

    @pl.when(jnp.logical_and(outer == 1, group_first))
    def _():
        pl.semaphore_wait(barrier, signals)

    @pl.when(jnp.logical_and(outer == 1, not_group))
    def _():
        pl.semaphore_wait(barrier, signals + 1)

    @pl.when(outer == 1)
    def _():
        crossing().start()

    own_aug[...] = augmented(packet[...], True).astype(BF16)

    @pl.when(outer == 1)
    def _():
        crossing().wait_recv()

    @pl.when(outer == 0)
    def _():
        origin[...] = packet[...]

    @pl.when(group_first)
    def _():
        packets[0] = origin[...]

    @pl.when(not_group)
    def _():
        near_copy(0).start()

    for k in range(1, NEAR):
        near_copy(k).start()


    def rows(k):
        return pl.ds(pl.multiple_of(k * BLOCK, BLOCK), BLOCK)

    def held(k, q):
        return pl.ds(pl.multiple_of((q * NEAR + k) * WIDTH, WIDTH), WIDTH)

    def fetch(k):
        @pl.when(jnp.logical_not(jnp.logical_and(group_first, k == 0)))
        def _():
            copy(packets.at[k], packets.at[k], send_near.at[k], recv_near.at[k], rep_peer(1)).wait_recv()

        remote_aug[rows(k), :] = augmented(packets[k], False).astype(BF16).T

    def values(dist):
        dist = jnp.maximum(dist, TINY)
        t = dist * lax.rsqrt(dist)
        value = ((t + LINEAR) * t + CONST) * jnp.exp2(-t)
        lead = value.astype(BF16)
        return lead, (value - lead.astype(F32)).astype(BF16)

    def build_whole(k, total):
        vector = two_terms(packets[k, 4:8] * OUTER)
        lead, rest = values(matmul(remote_aug[rows(k), :], own_aug[...]))
        for q in range(PARTS):
            high[held(k, q), :] = lead[q * WIDTH:(q + 1) * WIDTH]
            low[held(k, q), :] = rest[q * WIDTH:(q + 1) * WIDTH]
        fetch(k + 1)
        return total + matmul(vector, lead) + matmul(vector, rest)

    zeros = jnp.zeros((16, BLOCK), F32)
    fetch(0)
    partial[...] = lax.fori_loop(0, WHOLE, build_whole, zeros)
    for k in range(WHOLE + 1, NEAR):
        fetch(k)

    def image_part(q):
        for k in range(1, REPS):
            part_copy(q, k).wait_recv()
        whole = part1[q, 0]
        for other in range(1, REPS):
            whole = whole + part1[q, other]
        cols = pl.ds(pl.multiple_of(q * WIDTH, WIDTH), WIDTH)
        image1[q] = whole + noise[:, cols] * right[:, cols]

        @pl.when(own_first)
        def _():
            images[q, 0] = image1[q]

        @pl.when(not_own)
        def _():
            image_copy(q, 0).start()

        for k in range(1, NEAR):
            image_copy(q, k).start()

    def build_part(q, _):
        cols = pl.ds(pl.multiple_of(q * WIDTH, WIDTH), WIDTH)
        total = partial[:, cols]
        own = own_aug[:, cols]
        for k in range(WHOLE, NEAR):
            vector = two_terms(packets[k, 4:8] * OUTER)
            lead, rest = values(matmul(remote_aug[rows(k), :], own))
            for part in range(PARTS):
                high[held(k, part), cols] = lead[part * WIDTH:(part + 1) * WIDTH]
                low[held(k, part), cols] = rest[part * WIDTH:(part + 1) * WIDTH]
            total = total + matmul(vector, lead) + matmul(vector, rest)
        part1[q, rep] = total[0:4] + total[4:8]
        for k in range(1, REPS):
            part_copy(q, k).start()

        @pl.when(q >= 2)
        def _():
            image_part(q - 2)

        return 0

    lax.fori_loop(0, PARTS, build_part, 0)
    image_part(PARTS - 2)
    image_part(PARTS - 1)

    def again(n, total):
        q, first = n // 2, n % 2 * 4

        @pl.when(jnp.logical_not(jnp.logical_and(own_first, first == 0)))
        def _():
            arrived(q, first)

        for k in range(1, 4):
            arrived(q, first + k)
        vector = two_terms(jnp.concatenate([images[q, first + k] for k in range(4)], axis=1) * OUTER)
        part = rows(n)
        return total + matmul(vector, high[part, :]) + matmul(vector, low[part, :])

    def arrived(q, k):
        copy(images.at[q, k], images.at[q, k], send_image.at[q, k], recv_image.at[q, k], rep_peer(1)).wait_recv()

    total = lax.fori_loop(0, 2 * PARTS, again, zeros)
    own_part = total[0:4] + total[4:8]
    r0 = right[...]
    w1 = jnp.concatenate([image1[q] for q in range(PARTS)], axis=1)
    spread = noise[...] * w1

    lane = lax.broadcasted_iota(jnp.int32, (4, 128), 1)
    once = jnp.where(rep == 0, 1.0, 0.0)
    mine = own_part + once * spread
    grams = jnp.zeros((4, 128), F32)
    for at, product in enumerate((once * r0 * r0, once * r0 * w1, once * w1 * w1, r0 * mine, w1 * mine)):
        grams = jnp.where(lane == at, jnp.sum(product, axis=1, keepdims=True), grams)

    def over(slots, me, stage, peer, value):
        slots[me] = value
        copies = [
            copy(slots.at[me], slots.at[me], send_end.at[stage, k], recv_end.at[stage, k], peer(k)) for k in range(1, 8)
        ]
        for one in copies:
            one.start()
        return copies

    def added(slots, copies):
        for one in copies:
            one.wait_recv()
        value = slots[0]
        for other in range(1, 8):
            value = value + slots[other]
        return value

    across = lax.axis_index("blk") % 8
    first = over(sums_rep, rep, 0, rep_peer, grams)
    bulk = over(part2, rep, 3, rep_peer, own_part)
    second = over(sums_y, y, 1, y_peer, added(sums_rep, first))
    third = over(sums_zx, across, 2, zx_peer, added(sums_y, second))
    w2 = added(part2, bulk) + spread
    grams = added(sums_zx, third)

    g00, g01, g11, g02, g12 = (grams[:, at:at + 1] for at in range(5))
    alpha = g00 / g01
    new = g00 - 2.0 * alpha * g01 + alpha * alpha * g11
    more = 1.0 + new / g00
    bottom = more * more * g01 - alpha * more * (g02 + g11) + alpha * alpha * g12
    alpha2 = new / bottom
    direction = more * r0 - alpha * w1
    image = more * w1 - alpha * w2
    out[0:4] = alpha * r0 + alpha2 * direction
    out[4:8] = (r0 - alpha * w1) - alpha2 * image

    @pl.when(outer == 1)
    def _():
        crossing().wait_send()

    @pl.when(not_group)
    def _():
        near_copy(0).wait_send()

    for k in range(1, NEAR):
        near_copy(k).wait_send()
    for one in first + second + third + bulk:
        one.wait_send()

    def left(q, _):
        @pl.when(not_own)
        def _():
            image_copy(q, 0).wait_send()

        for k in range(1, NEAR):
            image_copy(q, k).wait_send()
        for k in range(1, REPS):
            part_copy(q, k).wait_send()
        return 0

    lax.fori_loop(0, PARTS, left, 0)


def local(coords, noise, right_side):
    vmem = pl.BlockSpec(memory_space=pltpu.VMEM)
    field = jax.ShapeDtypeStruct((8, BLOCK), F32)
    call = pl.pallas_call(
        kernel,
        out_shape=field,
        in_specs=[pl.BlockSpec(memory_space=pl.ANY)] * 3,
        out_specs=vmem,
        scratch_shapes=[
            pltpu.VMEM((8, BLOCK), F32),
            pltpu.VMEM((8, BLOCK), F32),
            pltpu.VMEM((NEAR, 8, BLOCK), F32),
            pltpu.VMEM((NEAR * BLOCK, BLOCK), BF16),
            pltpu.VMEM((NEAR * BLOCK, BLOCK), BF16),
            pltpu.VMEM((128, BLOCK), BF16),
            pltpu.VMEM((NEAR * BLOCK, 128), BF16),
            pltpu.VMEM((16, BLOCK), F32),
            pltpu.VMEM((PARTS, REPS, 4, WIDTH), F32),
            pltpu.VMEM((PARTS, 4, WIDTH), F32),
            pltpu.VMEM((PARTS, NEAR, 4, WIDTH), F32),
            pltpu.VMEM((REPS, 4, BLOCK), F32),
            pltpu.VMEM((REPS, 4, 128), F32),
            pltpu.VMEM((8, 4, 128), F32),
            pltpu.VMEM((8, 4, 128), F32),
            pltpu.SemaphoreType.DMA((NEAR + 1,)),
            pltpu.SemaphoreType.DMA((NEAR + 1,)),
            pltpu.SemaphoreType.DMA((PARTS, REPS)),
            pltpu.SemaphoreType.DMA((PARTS, REPS)),
            pltpu.SemaphoreType.DMA((PARTS, NEAR)),
            pltpu.SemaphoreType.DMA((PARTS, NEAR)),
            pltpu.SemaphoreType.DMA((4, 8)),
            pltpu.SemaphoreType.DMA((4, 8)),
            pltpu.VMEM((3, BLOCK), F32),
            pltpu.VMEM((1, BLOCK), F32),
            pltpu.VMEM((4, BLOCK), F32),
            pltpu.SemaphoreType.DMA((3,)),
        ],
        compiler_params=pltpu.CompilerParams(
            collective_id=0, has_side_effects=True, vmem_limit_bytes=60 * 1024 * 1024
        ),
    )
    both = call(coords, noise[None, :], right_side)
    return both[0:4], both[4:8]


def solution(mesh):
    return jax.shard_map(
        local,
        mesh=mesh,
        in_specs=(P(None, "blk"), P("blk"), P(None, "blk")),
        out_specs=(P(None, "blk"), P(None, "blk")),
        check_vma=False,
    )
```

time: 76.8 us -> 72.1 us (0.939)
  Pallas kernels: 74 us -> 69.7 us
    pallas_call x1, Pallas kernels: 74 us -> 69.7 us  [local(): both = call(coords, noise[None, :], right_side)]
    unnamed x4 -> x0, local copies, waits for them, and re-layouts: 1.94 us -> none
    slice x0 -> x1, local copies, waits for them, and re-layouts: none -> 1.45 us  [local(): return (both[0:4], both[4:8])]
where the time goes in v2:
time: 72.1 us; the launch traced here: 71.8 us
  Pallas kernels  69.7 us (97%)
  local copies, waits for them, and re-layouts  1.45 us (2%)
    pallas_call x1, Pallas kernels, local(): both = call(coords, noise[None, :], right_side)  69.7 us
    slice x1, local copies, waits for them, and re-layouts, local(): return (both[0:4], both[4:8])  1.45 us

profile of v2, /device:TPU:1, one launch (start us, length us, event | category | flops | bytes accessed | tf_op | source)
XLA Modules:
  0.0 71.8 jit_solution(9979091758836883156)
XLA Ops:
  0.6 69.7 %shard_map.50 = f32[8,1024]{1,0:T(8,128)} custom-call(f32[3,1024]{1,0:T(4,128)} %coords_in.1, f32[1,1024]{1,0:T(1,128)} %bitcast.1, f32[4,1024]{1,0:T(4,128)} %right_in.1), custom_call_target="tpu_custom_call" | custom-call | tf_op jit(solution)/shard_map/pallas_call | solution.py:427
  70.4 1.5 %fusion = (f32[4,1024]{1,0:T(4,128)}, f32[4,1024]{1,0:T(4,128)}) fusion(f32[8,1024]{1,0:T(8,128)} %shard_map.50), kind=kLoop, calls=%fused_computation | loop fusion | bytes 65536 | tf_op jit(solution)/shard_map/slice | solution.py:428

commit v3 on v2

--- a/solution.py
+++ b/solution.py
@@ -21,7 +21,7 @@
 
 BLOCK = 1024
 NEAR = 8
-WHOLE = 4
+WHOLE = 6
 PARTS = 4
 WIDTH = BLOCK // PARTS
 REPS = 8
@@ -38,19 +38,19 @@
     return ((y * 2 + zh) * 4 + x, zl * 2 + c)
 
 
-def partner(k, sign, relayed=False):
+def partner(k, sign):
     y, zh, x, zl, c = place()
-    outer = 0 if relayed else 1 - ((zl + 1) // 2) % 2
+    outer = 1 - ((zl + 1) // 2) % 2
     other_zl = zl + outer * (3 - 2 * zl)
     other_zh = zh + outer * (1 - 2 * zh)
     reader = zl if sign > 0 else other_zl
-    dx = (reader // 2 * 2 + c + k) % 4
+    dx = (reader // 2 * 2 + c) % 4
     return device((y + sign * DY[k] + 8) % 8, other_zh, (x + sign * dx + 4) % 4, other_zl, c)
 
 
-def over_border():
+def y_neighbour(step):
     y, zh, x, zl, c = place()
-    return device(y, 1 - zh, x, 3 - zl, c)
+    return device((y + step + 8) % 8, zh, x, zl, c)
 
 
 def rep_peer(k):
@@ -110,16 +110,13 @@
     return jnp.dot(a, b, preferred_element_type=F32)
 
 
-def kernel(coords_in, noise_in, right_in, out, packet, origin, packets, high, low, own_aug, remote_aug, partial, part1,
+def kernel(coords_in, noise_in, right_in, out, packet, packets, high, low, own_aug, remote_aug, partial, part1,
            image1, images, part2, sums_rep, sums_y, sums_zx, send_near, recv_near, send1, recv1, send_image, recv_image,
            send_end, recv_end, coords, noise, right, load):
     y, zh, x, zl, c = place()
     rep = lax.axis_index("rep")
     own_first = jnp.logical_and(zl == 1, c == 0)
     not_own = jnp.logical_not(own_first)
-    outer = 1 - ((zl + 1) // 2) % 2
-    group_first = zl // 2 * 2 + c == 0
-    not_group = jnp.logical_not(group_first)
 
     def copy(src, dst, sent, received, to):
         return pltpu.make_async_remote_copy(
@@ -127,16 +124,12 @@
         )
 
     barrier = pltpu.get_barrier_semaphore()
-    @pl.when(outer == 1)
+    for step in (1, -1):
+        pl.semaphore_signal(barrier, inc=1, device_id=y_neighbour(step), device_id_type=MESH)
+
+    @pl.when(not_own)
     def _():
-        pl.semaphore_signal(barrier, inc=1, device_id=over_border(), device_id_type=MESH)
-
-    for k in range(1, NEAR):
-        pl.semaphore_signal(barrier, inc=1, device_id=partner(k, 1, True), device_id_type=MESH)
-
-    @pl.when(not_group)
-    def _():
-        pl.semaphore_signal(barrier, inc=1, device_id=partner(0, 1, True), device_id_type=MESH)
+        pl.semaphore_signal(barrier, inc=1, device_id=partner(0, 1), device_id_type=MESH)
 
     for k in range(1, REPS):
         pl.semaphore_signal(barrier, inc=1, device_id=rep_peer(k), device_id_type=MESH)
@@ -155,8 +148,16 @@
     packet[3:4] = jnp.sum(centred * centred, axis=0, keepdims=True)
     packet[4:8] = right[...]
 
-    def near_copy(k):
-        return copy(origin, packets.at[k], send_near.at[k], recv_near.at[k], partner(k, -1, True))
+    def first_copy():
+        return copy(packet, packets.at[0], send_near.at[0], recv_near.at[0], partner(0, -1))
+
+    def turn_copy():
+        return copy(packets.at[0], packets.at[1], send_near.at[1], recv_near.at[1], y_neighbour(-1))
+
+    def ring_copy(k):
+        return copy(
+            packets.at[k], packets.at[k + 2], send_near.at[k + 2], recv_near.at[k + 2], y_neighbour(1 - 2 * (k % 2))
+        )
 
     def image_copy(q, k):
         return copy(image1.at[q], images.at[q, k], send_image.at[q, k], recv_image.at[q, k], partner(k, -1))
@@ -164,52 +165,17 @@
     def part_copy(q, k):
         return copy(part1.at[q, rep], part1.at[q, rep], send1.at[q, k], recv1.at[q, k], rep_peer(k))
 
-    def crossing():
-        return copy(packet, origin, send_near.at[NEAR], recv_near.at[NEAR], over_border())
-
-    signals = NEAR + REPS - 1
-
-    @pl.when(jnp.logical_and(outer == 0, group_first))
+    @pl.when(own_first)
     def _():
-        pl.semaphore_wait(barrier, signals - 1)
-
-    @pl.when(jnp.logical_and(outer == 0, not_group))
+        pl.semaphore_wait(barrier, REPS + 1)
+        packets[0] = packet[...]
+
+    @pl.when(not_own)
     def _():
-        pl.semaphore_wait(barrier, signals)
-
-    @pl.when(jnp.logical_and(outer == 1, group_first))
-    def _():
-        pl.semaphore_wait(barrier, signals)
-
-    @pl.when(jnp.logical_and(outer == 1, not_group))
-    def _():
-        pl.semaphore_wait(barrier, signals + 1)
-
-    @pl.when(outer == 1)
-    def _():
-        crossing().start()
+        pl.semaphore_wait(barrier, REPS + 2)
+        first_copy().start()
 
     own_aug[...] = augmented(packet[...], True).astype(BF16)
-
-    @pl.when(outer == 1)
-    def _():
-        crossing().wait_recv()
-
-    @pl.when(outer == 0)
-    def _():
-        origin[...] = packet[...]
-
-    @pl.when(group_first)
-    def _():
-        packets[0] = origin[...]
-
-    @pl.when(not_group)
-    def _():
-        near_copy(0).start()
-
-    for k in range(1, NEAR):
-        near_copy(k).start()
-
 
     def rows(k):
         return pl.ds(pl.multiple_of(k * BLOCK, BLOCK), BLOCK)
@@ -218,9 +184,17 @@
         return pl.ds(pl.multiple_of((q * NEAR + k) * WIDTH, WIDTH), WIDTH)
 
     def fetch(k):
-        @pl.when(jnp.logical_not(jnp.logical_and(group_first, k == 0)))
+        @pl.when(jnp.logical_not(jnp.logical_and(own_first, k == 0)))
         def _():
             copy(packets.at[k], packets.at[k], send_near.at[k], recv_near.at[k], rep_peer(1)).wait_recv()
+
+        @pl.when(k < NEAR - 2)
+        def _():
+            ring_copy(k).start()
+
+        @pl.when(k == 0)
+        def _():
+            turn_copy().start()
 
         remote_aug[rows(k), :] = augmented(packets[k], False).astype(BF16).T
 
@@ -241,10 +215,10 @@
         return total + matmul(vector, lead) + matmul(vector, rest)
 
     zeros = jnp.zeros((16, BLOCK), F32)
-    fetch(0)
+    fetch(jnp.int32(0))
     partial[...] = lax.fori_loop(0, WHOLE, build_whole, zeros)
     for k in range(WHOLE + 1, NEAR):
-        fetch(k)
+        fetch(jnp.int32(k))
 
     def image_part(q):
         for k in range(1, REPS):
@@ -255,6 +229,9 @@
         cols = pl.ds(pl.multiple_of(q * WIDTH, WIDTH), WIDTH)
         image1[q] = whole + noise[:, cols] * right[:, cols]
 
+        for k in range(NEAR - 1, 0, -1):
+            image_copy(q, k).start()
+
         @pl.when(own_first)
         def _():
             images[q, 0] = image1[q]
@@ -262,9 +239,6 @@
         @pl.when(not_own)
         def _():
             image_copy(q, 0).start()
-
-        for k in range(1, NEAR):
-            image_copy(q, k).start()
 
     def build_part(q, _):
         cols = pl.ds(pl.multiple_of(q * WIDTH, WIDTH), WIDTH)
@@ -281,15 +255,11 @@
         for k in range(1, REPS):
             part_copy(q, k).start()
 
-        @pl.when(q >= 2)
-        def _():
-            image_part(q - 2)
-
         return 0
 
     lax.fori_loop(0, PARTS, build_part, 0)
-    image_part(PARTS - 2)
-    image_part(PARTS - 1)
+    for q in range(PARTS):
+        image_part(q)
 
     def again(n, total):
         q, first = n // 2, n % 2 * 4
@@ -356,16 +326,13 @@
     out[0:4] = alpha * r0 + alpha2 * direction
     out[4:8] = (r0 - alpha * w1) - alpha2 * image
 
-    @pl.when(outer == 1)
+    @pl.when(not_own)
     def _():
-        crossing().wait_send()
-
-    @pl.when(not_group)
-    def _():
-        near_copy(0).wait_send()
-
-    for k in range(1, NEAR):
-        near_copy(k).wait_send()
+        first_copy().wait_send()
+
+    turn_copy().wait_send()
+    for k in range(NEAR - 2):
+        ring_copy(k).wait_send()
     for one in first + second + third + bulk:
         one.wait_send()
 
@@ -392,7 +359,6 @@
         in_specs=[pl.BlockSpec(memory_space=pl.ANY)] * 3,
         out_specs=vmem,
         scratch_shapes=[
-            pltpu.VMEM((8, BLOCK), F32),
             pltpu.VMEM((8, BLOCK), F32),
             pltpu.VMEM((NEAR, 8, BLOCK), F32),
             pltpu.VMEM((NEAR * BLOCK, BLOCK), BF16),
@@ -407,8 +373,8 @@
             pltpu.VMEM((REPS, 4, 128), F32),
             pltpu.VMEM((8, 4, 128), F32),
             pltpu.VMEM((8, 4, 128), F32),
-            pltpu.SemaphoreType.DMA((NEAR + 1,)),
-            pltpu.SemaphoreType.DMA((NEAR + 1,)),
+            pltpu.SemaphoreType.DMA((NEAR,)),
+            pltpu.SemaphoreType.DMA((NEAR,)),
             pltpu.SemaphoreType.DMA((PARTS, REPS)),
             pltpu.SemaphoreType.DMA((PARTS, REPS)),
             pltpu.SemaphoreType.DMA((PARTS, NEAR)),

time: 72.1 us -> 70.6 us (0.979)
  Pallas kernels: 69.7 us -> 68.2 us
    pallas_call x1, Pallas kernels: 69.7 us -> 68.2 us  [local(): both = call(coords, noise[None, :], right_side)]
where the time goes in v3:
time: 70.6 us; the launch traced here: 70.3 us
  Pallas kernels  68.2 us (97%)
  local copies, waits for them, and re-layouts  1.45 us (2%)
    pallas_call x1, Pallas kernels, local(): both = call(coords, noise[None, :], right_side)  68.2 us
    slice x1, local copies, waits for them, and re-layouts, local(): return (both[0:4], both[4:8])  1.45 us

profile of v3, /device:TPU:1, one launch (start us, length us, event | category | flops | bytes accessed | tf_op | source)
XLA Modules:
  0.0 70.3 jit_solution(13168065757184738365)
XLA Ops:
  0.6 68.2 %shard_map.50 = f32[8,1024]{1,0:T(8,128)} custom-call(f32[3,1024]{1,0:T(4,128)} %coords_in.1, f32[1,1024]{1,0:T(1,128)} %bitcast.1, f32[4,1024]{1,0:T(4,128)} %right_in.1), custom_call_target="tpu_custom_call" | custom-call | tf_op jit(solution)/shard_map/pallas_call | solution.py:393
  68.9 1.5 %fusion = (f32[4,1024]{1,0:T(4,128)}, f32[4,1024]{1,0:T(4,128)}) fusion(f32[8,1024]{1,0:T(8,128)} %shard_map.50), kind=kLoop, calls=%fused_computation | loop fusion | bytes 65536 | tf_op jit(solution)/shard_map/slice | solution.py:394

commit v4 on v3

--- a/solution.py
+++ b/solution.py
@@ -310,9 +310,31 @@
     across = lax.axis_index("blk") % 8
     first = over(sums_rep, rep, 0, rep_peer, grams)
     bulk = over(part2, rep, 3, rep_peer, own_part)
+    @pl.when(not_own)
+    def _():
+        first_copy().wait_send()
+
+    turn_copy().wait_send()
+    for k in range(NEAR - 2):
+        ring_copy(k).wait_send()
+    def left(q, _):
+        @pl.when(not_own)
+        def _():
+            image_copy(q, 0).wait_send()
+
+        for k in range(1, NEAR):
+            image_copy(q, k).wait_send()
+        for k in range(1, REPS):
+            part_copy(q, k).wait_send()
+        return 0
+
+    lax.fori_loop(0, PARTS, left, 0)
+
     second = over(sums_y, y, 1, y_peer, added(sums_rep, first))
     third = over(sums_zx, across, 2, zx_peer, added(sums_y, second))
     w2 = added(part2, bulk) + spread
+    for one in first + bulk + second:
+        one.wait_send()
     grams = added(sums_zx, third)
 
     g00, g01, g11, g02, g12 = (grams[:, at:at + 1] for at in range(5))
@@ -325,29 +347,8 @@
     image = more * w1 - alpha * w2
     out[0:4] = alpha * r0 + alpha2 * direction
     out[4:8] = (r0 - alpha * w1) - alpha2 * image
-
-    @pl.when(not_own)
-    def _():
-        first_copy().wait_send()
-
-    turn_copy().wait_send()
-    for k in range(NEAR - 2):
-        ring_copy(k).wait_send()
-    for one in first + second + third + bulk:
+    for one in third:
         one.wait_send()
-
-    def left(q, _):
-        @pl.when(not_own)
-        def _():
-            image_copy(q, 0).wait_send()
-
-        for k in range(1, NEAR):
-            image_copy(q, k).wait_send()
-        for k in range(1, REPS):
-            part_copy(q, k).wait_send()
-        return 0
-
-    lax.fori_loop(0, PARTS, left, 0)
 
 
 def local(coords, noise, right_side):

time: 70.6 us -> 70.4 us (level)
  no operation moved by 1% of the time
where the time goes in v4:
time: 70.4 us; the launch traced here: 70.2 us
  Pallas kernels  68.1 us (97%)
  local copies, waits for them, and re-layouts  1.45 us (2%)
    pallas_call x1, Pallas kernels, local(): both = call(coords, noise[None, :], right_side)  68.1 us
    slice x1, local copies, waits for them, and re-layouts, local(): return (both[0:4], both[4:8])  1.45 us

profile of v4, /device:TPU:1, one launch (start us, length us, event | category | flops | bytes accessed | tf_op | source)
XLA Modules:
  0.0 70.2 jit_solution(13591872563545089014)
XLA Ops:
  0.6 68.1 %shard_map.50 = f32[8,1024]{1,0:T(8,128)} custom-call(f32[3,1024]{1,0:T(4,128)} %coords_in.1, f32[1,1024]{1,0:T(1,128)} %bitcast.1, f32[4,1024]{1,0:T(4,128)} %right_in.1), custom_call_target="tpu_custom_call" | custom-call | tf_op jit(solution)/shard_map/pallas_call | solution.py:394
  68.7 1.5 %fusion = (f32[4,1024]{1,0:T(4,128)}, f32[4,1024]{1,0:T(4,128)}) fusion(f32[8,1024]{1,0:T(8,128)} %shard_map.50), kind=kLoop, calls=%fused_computation | loop fusion | bytes 65536 | tf_op jit(solution)/shard_map/slice | solution.py:395
